TPU v7x, 512 devices: a whole 4x4x16 slice. The times are simulated.
512 devices in a mesh: slab: 64 (over z, x_lo, core), mode: 8 (over x_hi, y).
Axes of the slice: x: 4 (x_hi: 2, x_lo: 2; x = x_hi * 2 + x_lo), y: 4, z: 16, core: 2. Of those that a mesh axis runs over, the one named last changes fastest.
Arguments:
- initial_block: bfloat16 [96, 64, 64, 128], P('mode', 'slab'), may hold values from -180 to 180
- labels: int32 [64, 64, 128], P('slab'), may hold values from 0 to 3
- filter_low: float32 [], replicated, may hold values from 1 to 3
- filter_high: float32 [], replicated, may hold values from 22 to 24
Outputs:
- modes_out: bfloat16 [96, 64, 64, 128], P('mode', 'slab')
- projected: float32 [96, 96], replicated
Inputs may be any that keep to these rules, and one draw needn't show every extreme that they name: `labels`: 0 marks a voxel outside the brain; 1, 2 and 3 are tissue classes.
All inputs are finite; a program needn't handle non-finite values.
Results may differ from a plain program's by a relative error of at most 0.0015.
The roundings to bfloat16 on the way count: a program that leaves them out, or rounds other values in their place, can miss the bound.
Values may be sent and summed in bfloat16 or wider, within the bound.
No kernel may reach another device: no remote copies, remote signals or barrier semaphores. Data moves between devices by JAX's collectives and lax.ppermute only.
A program may use at most 64 MiB of HBM per device.

v0:
```python
import math
import jax
import jax.numpy as jnp
from jax import lax
from jax.sharding import PartitionSpec as P

DEGREE = 4
ROOTS = (0.0, 0.7745967, 1.0, 1.3416408)


def padded_2(shard, sides, width):
    for axis, dim in sides:
        peers, length = (lax.axis_size(axis), shard.shape[dim])
        up = [(i, (i + 1) % peers) for i in range(peers - 1)]
        down = [(j, i) for i, j in up]
        last = lax.slice_in_dim(shard, length - width, length, axis=dim)
        first = lax.slice_in_dim(shard, 0, width, axis=dim)
        before = lax.ppermute(last, axis, up)
        after = lax.ppermute(first, axis, down)
        shard = jnp.concatenate([before, shard, after], axis=dim)
    return shard


def strength_of(labels):
    total = jnp.zeros(labels.shape, jnp.float32)
    for level in range(1, 4):
        total = total + jnp.where(labels == level, ROOTS[level], 0.0)
    return total


def face_weights(strong, padded):
    return (
        strong * padded[:-2, 1:-1, 1:-1],
        strong * padded[2:, 1:-1, 1:-1],
        strong * padded[1:-1, :-2, 1:-1],
        strong * padded[1:-1, 2:, 1:-1],
        strong * padded[1:-1, 1:-1, :-2],
        strong * padded[1:-1, 1:-1, 2:],
    )


def combine_faces(field, padded, weights):
    beside_all = (
        padded[:, :-2, 1:-1, 1:-1],
        padded[:, 2:, 1:-1, 1:-1],
        padded[:, 1:-1, :-2, 1:-1],
        padded[:, 1:-1, 2:, 1:-1],
        padded[:, 1:-1, 1:-1, :-2],
        padded[:, 1:-1, 1:-1, 2:],
    )
    total = weights[0] * (field - beside_all[0])
    for weight, other in zip(weights[1:], beside_all[1:]):
        total = total + weight * (field - other)
    return total


def chebyshev(block, apply_fn, low, high):
    centre = 0.5 * (high + low)
    half = 0.5 * (high - low)
    prev = block
    cur = (apply_fn(block) - centre * block) / half
    for step in range(DEGREE - 1):
        nxt = 2.0 * (apply_fn(cur) - centre * cur) / half - prev
        prev, cur = (cur, nxt)
    return cur


def factor(gram, cross):
    lower = jnp.linalg.cholesky(gram)
    inverse = jax.scipy.linalg.solve_triangular(
        lower, jnp.eye(gram.shape[0], dtype=jnp.float32), lower=True
    )
    projected = jnp.dot(
        jnp.dot(inverse, cross, precision=lax.Precision.HIGHEST),
        inverse.T,
        precision=lax.Precision.HIGHEST,
    )
    return (projected, inverse.T.astype(jnp.bfloat16))


def per_device(initial_block, labels, filter_low, filter_high):
    local = initial_block.shape[0]
    modes = local * lax.axis_size("mode")
    depth, height, width = labels.shape
    scale = math.sqrt(depth * height * width * lax.axis_size("slab"))
    strong = strength_of(labels)
    mask = (labels > 0).astype(jnp.float32)
    rim = padded_2(strong, (("slab", 0),), 1)
    weights = face_weights(strong, jnp.pad(rim, ((0, 0), (1, 1), (1, 1))))

    def apply_fn(field):
        padded = padded_2(field, (("slab", 1),), 1)
        return combine_faces(field, jnp.pad(padded, ((0, 0), (0, 0), (1, 1), (1, 1))), weights)

    block = initial_block.astype(jnp.float32) * mask[None]
    cur = chebyshev(block, apply_fn, filter_low, filter_high)
    filtered = cur.astype(jnp.bfloat16)
    applied = apply_fn(cur).astype(jnp.bfloat16)
    everything = lax.all_gather(filtered, "mode", axis=0, tiled=True)
    whole = everything.reshape(modes, -1)
    own = filtered.reshape(local, -1)
    own_applied = applied.reshape(local, -1)
    gram_block = jnp.einsum("mc,nc->mn", whole, own, preferred_element_type=jnp.float32)
    cross_block = jnp.einsum("mc,nc->mn", whole, own_applied, preferred_element_type=jnp.float32)
    gram_sum, cross_sum = lax.psum((gram_block, cross_block), "slab")
    gram, cross = (
        lax.all_gather(gram_sum, "mode", axis=1, tiled=True),
        lax.all_gather(cross_sum, "mode", axis=1, tiled=True),
    )
    projected, rotation = factor(gram, cross)
    columns = lax.dynamic_slice_in_dim(rotation, lax.axis_index("mode") * local, local, 1)
    turned = jnp.einsum("mj,mc->jc", columns, whole, preferred_element_type=jnp.float32)
    modes_out = (turned * scale).astype(jnp.bfloat16).reshape(local, depth, height, width)
    return (modes_out, projected)


def solution(mesh):
    placed = (P("mode", "slab", None, None), P("slab", None, None), P(), P())
    return jax.shard_map(
        per_device,
        mesh=mesh,
        in_specs=placed,
        out_specs=(P("mode", "slab", None, None), P()),
        check_vma=False,
    )
```

profile of v0, /device:TPU:4, one launch (start us, length us, event | category | flops | bytes accessed | tf_op | source)
XLA Modules:
  0.0 454.6 jit_solution(9304281027527931800)
XLA Ops:
  9.0 1.8 collective-permute-start.1
  10.8 1.3 collective-permute-start.3
  12.9 4.0 collective-permute-start
  16.9 1.3 collective-permute-start.2
  19.5 1.7 collective-permute-done.2
  23.5 4.6 %collective-permute-start.4 = (f32[12,1,64,128]{3,2,1,0:T(8,128)S(1)}, f32[12,1,64,128]{3,2,1,0:T(8,128)S(1)}, u32[]{:S(2)}, u32[]{:S(2)}) collective-permute-start(f32[12,1,64,128]{3,2,1,0:T(8,128)S(1)} %fusion.66), channel_id=1, source_target_pairs={{0,8},{8,16},{16,24},{24,32},{32,40},{40,48},{48,56},{56,64},{64,7... | collective-permute-start | bytes 1179656 | tf_op jit(solution)/shard_map/ppermute | solution.py:18
  28.1 1.3 collective-permute-start.5
  29.4 3.0 collective-permute-done.5
  33.7 9.0 %collective-permute-start.6 = (f32[12,1,64,128]{3,2,1,0:T(8,128)S(1)}, f32[12,1,64,128]{3,2,1,0:T(8,128)S(1)}, u32[]{:S(2)}, u32[]{:S(2)}) collective-permute-start(f32[12,1,64,128]{3,2,1,0:T(8,128)S(1)} %fusion.56), channel_id=1, source_target_pairs={{0,8},{8,16},{16,24},{24,32},{32,40},{40,48},{48,56},{56,64},{64,7... | collective-permute-start | bytes 1179656 | tf_op jit(solution)/shard_map/ppermute | solution.py:18
  42.7 1.3 collective-permute-start.7
  44.0 2.3 collective-permute-done.7
  47.6 8.3 %collective-permute-start.8 = (f32[12,1,64,128]{3,2,1,0:T(8,128)S(1)}, f32[12,1,64,128]{3,2,1,0:T(8,128)S(1)}, u32[]{:S(2)}, u32[]{:S(2)}) collective-permute-start(f32[12,1,64,128]{3,2,1,0:T(8,128)S(1)} %fusion.44), channel_id=1, source_target_pairs={{0,8},{8,16},{16,24},{24,32},{32,40},{40,48},{48,56},{56,64},{64,7... | collective-permute-start | bytes 1179656 | tf_op jit(solution)/shard_map/ppermute | solution.py:18
  57.2 2.3 collective-permute-done.9
  61.5 8.3 %collective-permute-start.10 = (f32[12,1,64,128]{3,2,1,0:T(8,128)S(1)}, f32[12,1,64,128]{3,2,1,0:T(8,128)S(1)}, u32[]{:S(2)}, u32[]{:S(2)}) collective-permute-start(f32[12,1,64,128]{3,2,1,0:T(8,128)S(1)} %get-tuple-element.11), channel_id=1, source_target_pairs={{0,8},{8,16},{16,24},{24,32},{32,40},{40,48},{48,56},{56,64},{64,7... | collective-permute-start | bytes 1179656 | tf_op jit(solution)/shard_map/ppermute | solution.py:18
  69.8 1.3 collective-permute-start.11
  71.1 2.3 collective-permute-done.11
  74.7 67.0 %all-gather.4.cloned.1.call-done = bf16[96,1,64,128]{3,2,1,0:T(8,128)(2,1)} async-done(((bf16[12,1,64,128]{3,2,1,0:T(8,128)(2,1)}), bf16[96,1,64,128]{3,2,1,0:T(8,128)(2,1)}) %all-gather.4.cloned.1.call-update) | async-done | bytes 1572880 | tf_op jit(solution)/shard_map/all_gather | solution.py:99
  141.7 2.6 fusion.15
  144.3 2.4 fusion.12
  146.7 212.0 %all-reduce.6 = (f32[96,12]{0,1:T(8,128)S(1)}, f32[96,12]{0,1:T(8,128)S(1)}) all-reduce(f32[96,12]{0,1:T(8,128)S(1)} %fusion.12, f32[96,12]{0,1:T(8,128)S(1)} %fusion.15), channel_id=1, replica_groups=mesh['slab'=64,'mode'=8] {'slab'}, use_global_device_ids=true, to_apply=%region_0.1 | all-reduce | flops 2304 | bytes 18432 | tf_op jit(solution)/shard_map/psum | solution.py:105
  358.7 34.3 %all-gather = f32[8,12,96]{2,1,0:T(8,128)S(1)} all-gather(f32[1,12,96]{2,1,0:T(8,128)S(1)} %bitcast.67), channel_id=1, replica_groups=mesh['slab'=64,'mode'=8] {'mode'}, dimensions={0}, use_global_device_ids=true | all-gather | bytes 41472 | tf_op jit(solution)/shard_map/all_gather | solution.py:107
  393.1 8.8 %cholesky.17 = f32[96,96]{1,0:T(8,128)S(1)} custom-call(f32[96,96]{1,0:T(8,128)S(1)} %fusion.82), custom_call_target="Cholesky" | custom-call | tf_op jit(solution)/shard_map/jit(cholesky)/cholesky | solution.py:69
  403.2 7.4 %custom-call.7 = f32[1,96,96]{1,2,0:T(8,128)S(1)} custom-call(f32[1,96,96]{2,1,0:T(8,128)S(1)} %fusion.79), custom_call_target="InvertDiagBlocksLowerTriangular" | custom-call | tf_op jit(solution)/shard_map/jit(_solve_triangular)/triangular_solve | solution.py:70
  410.8 34.2 %all-gather.1 = f32[8,12,96]{2,1,0:T(8,128)S(1)} all-gather(f32[1,12,96]{2,1,0:T(8,128)S(1)} %bitcast.66), channel_id=1, replica_groups=mesh['slab'=64,'mode'=8] {'mode'}, dimensions={0}, use_global_device_ids=true | all-gather | bytes 41472 | tf_op jit(solution)/shard_map/all_gather | solution.py:108
  (44 shorter events, 16.3 us)
Async XLA Ops:
  7.2 134.5 %all-gather.4.cloned.1.call-start = ((), (), s32[]{:S(2)}) async-start(), calls=%async_computation | async-start | bytes 1769472 | tf_op jit(solution)/shard_map/all_gather | solution.py:99
  8.0 15.0 %copy-start = (bf16[12,1,64,128]{3,2,1,0:T(8,128)(2,1)S(1)}, bf16[12,1,64,128]{3,2,1,0:T(8,128)(2,1)}, u32[]{:S(2)}) copy-start(bf16[12,1,64,128]{3,2,1,0:T(8,128)(2,1)} %param.4) | copy-start | bytes 589828
  9.0 13.2 %collective-permute-start.1 = (f32[12,1,64,128]{3,2,1,0:T(8,128)S(1)}, f32[12,1,64,128]{3,2,1,0:T(8,128)S(1)}, u32[]{:S(2)}, u32[]{:S(2)}) collective-permute-start(f32[12,1,64,128]{3,2,1,0:T(8,128)S(1)} %convert_multiply_fusion), channel_id=1, source_target_pairs={{0,8},{8,16},{16,24},{24,32},{32,40},{40,48},{48,56},{56,64},{64,7... | collective-permute-start | bytes 1179656 | tf_op jit(solution)/shard_map/ppermute | solution.py:18
  10.8 11.4 %collective-permute-start.3 = (f32[12,1,64,128]{3,2,1,0:T(8,128)S(1)}, f32[12,1,64,128]{3,2,1,0:T(8,128)S(1)}, u32[]{:S(2)}, u32[]{:S(2)}) collective-permute-start(f32[12,1,64,128]{3,2,1,0:T(8,128)S(1)} %convert_multiply_fusion), channel_id=1, source_target_pairs={{8,0},{16,8},{24,16},{32,24},{40,32},{48,40},{56,48},{64,56},{72,6... | collective-permute-start | bytes 1179656 | tf_op jit(solution)/shard_map/ppermute | solution.py:19
  12.9 6.6 %collective-permute-start = (f32[1,64,128]{2,1,0:T(8,128)S(1)}, f32[1,64,128]{2,1,0:T(8,128)S(1)}, u32[]{:S(2)}, u32[]{:S(2)}) collective-permute-start(f32[1,64,128]{2,1,0:T(8,128)S(1)} %select_add_fusion), channel_id=1, source_target_pairs={{0,8},{8,16},{16,24},{24,32},{32,40},{40,48},{48,56},{56,64},{64,7... | collective-permute-start | bytes 98312 | tf_op jit(solution)/shard_map/ppermute | solution.py:18
  16.9 4.3 collective-permute-start.2
  23.5 5.9 %collective-permute-start.4 = (f32[12,1,64,128]{3,2,1,0:T(8,128)S(1)}, f32[12,1,64,128]{3,2,1,0:T(8,128)S(1)}, u32[]{:S(2)}, u32[]{:S(2)}) collective-permute-start(f32[12,1,64,128]{3,2,1,0:T(8,128)S(1)} %fusion.66), channel_id=1, source_target_pairs={{0,8},{8,16},{16,24},{24,32},{32,40},{40,48},{48,56},{56,64},{64,7... | collective-permute-start | bytes 1179656 | tf_op jit(solution)/shard_map/ppermute | solution.py:18
  28.1 4.3 collective-permute-start.5
  33.7 10.3 %collective-permute-start.6 = (f32[12,1,64,128]{3,2,1,0:T(8,128)S(1)}, f32[12,1,64,128]{3,2,1,0:T(8,128)S(1)}, u32[]{:S(2)}, u32[]{:S(2)}) collective-permute-start(f32[12,1,64,128]{3,2,1,0:T(8,128)S(1)} %fusion.56), channel_id=1, source_target_pairs={{0,8},{8,16},{16,24},{24,32},{32,40},{40,48},{48,56},{56,64},{64,7... | collective-permute-start | bytes 1179656 | tf_op jit(solution)/shard_map/ppermute | solution.py:18
  42.7 3.6 collective-permute-start.7
  47.6 9.6 %collective-permute-start.8 = (f32[12,1,64,128]{3,2,1,0:T(8,128)S(1)}, f32[12,1,64,128]{3,2,1,0:T(8,128)S(1)}, u32[]{:S(2)}, u32[]{:S(2)}) collective-permute-start(f32[12,1,64,128]{3,2,1,0:T(8,128)S(1)} %fusion.44), channel_id=1, source_target_pairs={{0,8},{8,16},{16,24},{24,32},{32,40},{40,48},{48,56},{56,64},{64,7... | collective-permute-start | bytes 1179656 | tf_op jit(solution)/shard_map/ppermute | solution.py:18
  55.9 3.6 collective-permute-start.9
  61.5 9.6 %collective-permute-start.10 = (f32[12,1,64,128]{3,2,1,0:T(8,128)S(1)}, f32[12,1,64,128]{3,2,1,0:T(8,128)S(1)}, u32[]{:S(2)}, u32[]{:S(2)}) collective-permute-start(f32[12,1,64,128]{3,2,1,0:T(8,128)S(1)} %get-tuple-element.11), channel_id=1, source_target_pairs={{0,8},{8,16},{16,24},{24,32},{32,40},{40,48},{48,56},{56,64},{64,7... | collective-permute-start | bytes 1179656 | tf_op jit(solution)/shard_map/ppermute | solution.py:18
  69.8 3.6 collective-permute-start.11
  74.2 70.1 %copy-start.2 = (bf16[12,1,64,128]{3,2,1,0:T(8,128)(2,1)S(1)}, bf16[12,1,64,128]{3,2,1,0:T(8,128)(2,1)}, u32[]{:S(2)}) copy-start(bf16[12,1,64,128]{3,2,1,0:T(8,128)(2,1)} %get-tuple-element.10) | copy-start | bytes 589828
  141.7 304.4 %copy-start.1 = (bf16[96,1,64,128]{3,2,1,0:T(8,128)(2,1)S(1)}, bf16[96,1,64,128]{3,2,1,0:T(8,128)(2,1)}, u32[]{:S(2)}) copy-start(bf16[96,1,64,128]{3,2,1,0:T(8,128)(2,1)} %all-gather.4.cloned.1.call-done) | copy-start | bytes 4718596
Sparse Core Ops, SparseCore 0:
  61.6 80.0 all-gather.3
where the time goes:
time: 455 us
  blocking collectives  280 us (62%)
  waiting for transfers between devices  78.8 us (17%)
  starting transfers between devices  43.7 us (10%)
  other arithmetic  28 us (6%)
  between operations  15.6 us (3%)
  matrix products  7.25 us (2%)
    psum x1, blocking collectives, per_device(): gram_sum, cross_sum = lax.psum((gram_block, cross_block), 'slab')  212 us
    all_gather x1, waiting for transfers between devices, per_device(): everything = lax.all_gather(filtered, 'mode', axis=0, tiled=True)  67 us
    ppermute x6, starting transfers between devices, padded_2(): before = lax.ppermute(last, axis, up)  35.9 us
    all_gather x1, blocking collectives, per_device(): lax.all_gather(gram_sum, 'mode', axis=1, tiled=True)  34.3 us
    all_gather x1, blocking collectives, per_device(): lax.all_gather(cross_sum, 'mode', axis=1, tiled=True)  34.2 us
    ppermute x6, waiting for transfers between devices, padded_2(): after = lax.ppermute(first, axis, down)  11.7 us
    another operation x3, other arithmetic, factor(): lower = jnp.linalg.cholesky(gram)  9.45 us
  transfers between devices with their start and end apart: 13, of which 6 were waited for; matrix products, arithmetic and copies ran while one was open for 1% of the time, Pallas kernels for 0%

commit v1 on v0

--- a/solution.py
+++ b/solution.py
@@ -105,7 +105,12 @@
     gram_sum, cross_sum = lax.psum((gram_block, cross_block), "slab")
     gram, cross = (
         lax.all_gather(gram_sum, "mode", axis=1, tiled=True),
-        lax.all_gather(cross_sum, "mode", axis=1, tiled=True),
+        jnp.concatenate(
+            lax.all_to_all(
+                jnp.stack([cross_sum for _ in range(lax.axis_size("mode"))]), "mode", 0, 0
+            ),
+            1,
+        ),
     )
     projected, rotation = factor(gram, cross)
     columns = lax.dynamic_slice_in_dim(rotation, lax.axis_index("mode") * local, local, 1)

time: 455 us -> 432 us (0.949)
  the two profiles are of different devices: /device:TPU:4 before, /device:TPU:8 now
where the time goes in v1:
time: 432 us; the launch traced here: 431 us
  blocking collectives  243 us (56%)
  waiting for transfers between devices  85.2 us (20%)
  starting transfers between devices  50.9 us (12%)
  other arithmetic  28 us (6%)
  between operations  15.6 us (4%)
  matrix products  7.25 us (2%)
    psum x1, blocking collectives, per_device(): gram_sum, cross_sum = lax.psum((gram_block, cross_block), 'slab')  210 us
    all_gather x1, waiting for transfers between devices, per_device(): everything = lax.all_gather(filtered, 'mode', axis=0, tiled=True)  69.1 us
    ppermute x6, starting transfers between devices, padded_2(): before = lax.ppermute(last, axis, up)  36.2 us
    all_gather x1, blocking collectives, per_device(): lax.all_gather(gram_sum, 'mode', axis=1, tiled=True)  33.2 us
    ppermute x6, waiting for transfers between devices, padded_2(): after = lax.ppermute(first, axis, down)  11.4 us
    another operation x3, other arithmetic, factor(): lower = jnp.linalg.cholesky(gram)  9.45 us
  transfers between devices with their start and end apart: 14, of which 7 were waited for; matrix products, arithmetic and copies ran while one was open for 1% of the time, Pallas kernels for 0%

profile of v1, /device:TPU:8, one launch (start us, length us, event | category | flops | bytes accessed | tf_op | source)
XLA Modules:
  0.0 431.2 jit_solution(7965790386469745461)
XLA Ops:
  9.0 1.8 collective-permute-start.1
  10.8 1.3 collective-permute-start.3
  12.9 4.3 collective-permute-start
  17.1 1.3 collective-permute-start.2
  19.8 1.7 collective-permute-done.2
  23.8 4.6 %collective-permute-start.4 = (f32[12,1,64,128]{3,2,1,0:T(8,128)S(1)}, f32[12,1,64,128]{3,2,1,0:T(8,128)S(1)}, u32[]{:S(2)}, u32[]{:S(2)}) collective-permute-start(f32[12,1,64,128]{3,2,1,0:T(8,128)S(1)} %fusion.66), channel_id=1, source_target_pairs={{0,8},{8,16},{16,24},{24,32},{32,40},{40,48},{48,56},{56,64},{64,7... | collective-permute-start | bytes 1179656 | tf_op jit(solution)/shard_map/ppermute | solution.py:18
  28.3 1.3 collective-permute-start.5
  29.7 2.7 collective-permute-done.5
  33.7 9.0 %collective-permute-start.6 = (f32[12,1,64,128]{3,2,1,0:T(8,128)S(1)}, f32[12,1,64,128]{3,2,1,0:T(8,128)S(1)}, u32[]{:S(2)}, u32[]{:S(2)}) collective-permute-start(f32[12,1,64,128]{3,2,1,0:T(8,128)S(1)} %fusion.56), channel_id=1, source_target_pairs={{0,8},{8,16},{16,24},{24,32},{32,40},{40,48},{48,56},{56,64},{64,7... | collective-permute-start | bytes 1179656 | tf_op jit(solution)/shard_map/ppermute | solution.py:18
  42.7 1.3 collective-permute-start.7
  44.0 2.3 collective-permute-done.7
  47.6 8.3 %collective-permute-start.8 = (f32[12,1,64,128]{3,2,1,0:T(8,128)S(1)}, f32[12,1,64,128]{3,2,1,0:T(8,128)S(1)}, u32[]{:S(2)}, u32[]{:S(2)}) collective-permute-start(f32[12,1,64,128]{3,2,1,0:T(8,128)S(1)} %fusion.44), channel_id=1, source_target_pairs={{0,8},{8,16},{16,24},{24,32},{32,40},{40,48},{48,56},{56,64},{64,7... | collective-permute-start | bytes 1179656 | tf_op jit(solution)/shard_map/ppermute | solution.py:18
  57.2 2.3 collective-permute-done.9
  61.5 8.3 %collective-permute-start.10 = (f32[12,1,64,128]{3,2,1,0:T(8,128)S(1)}, f32[12,1,64,128]{3,2,1,0:T(8,128)S(1)}, u32[]{:S(2)}, u32[]{:S(2)}) collective-permute-start(f32[12,1,64,128]{3,2,1,0:T(8,128)S(1)} %get-tuple-element.11), channel_id=1, source_target_pairs={{0,8},{8,16},{16,24},{24,32},{32,40},{40,48},{48,56},{56,64},{64,7... | collective-permute-start | bytes 1179656 | tf_op jit(solution)/shard_map/ppermute | solution.py:18
  71.1 2.3 collective-permute-done.11
  74.7 69.1 %all-gather.3.cloned.1.call-done = bf16[96,1,64,128]{3,2,1,0:T(8,128)(2,1)} async-done(((bf16[12,1,64,128]{3,2,1,0:T(8,128)(2,1)}), bf16[96,1,64,128]{3,2,1,0:T(8,128)(2,1)}) %all-gather.3.cloned.1.call-update) | async-done | bytes 1572880 | tf_op jit(solution)/shard_map/all_gather | solution.py:99
  143.8 2.6 fusion.15
  146.3 2.4 fusion.12
  148.8 209.5 %all-reduce.6 = (f32[96,12]{0,1:T(8,128)S(1)}, f32[96,12]{0,1:T(8,128)S(1)}) all-reduce(f32[96,12]{0,1:T(8,128)S(1)} %fusion.12, f32[96,12]{0,1:T(8,128)S(1)} %fusion.15), channel_id=1, replica_groups=mesh['slab'=64,'mode'=8] {'slab'}, use_global_device_ids=true, to_apply=%region_0.1 | all-reduce | flops 2304 | bytes 18432 | tf_op jit(solution)/shard_map/psum | solution.py:105
  358.3 33.2 %all-gather = f32[8,12,96]{2,1,0:T(8,128)S(1)} all-gather(f32[1,12,96]{2,1,0:T(8,128)S(1)} %bitcast.67), channel_id=1, replica_groups=mesh['slab'=64,'mode'=8] {'mode'}, dimensions={0}, use_global_device_ids=true | all-gather | bytes 41472 | tf_op jit(solution)/shard_map/all_gather | solution.py:107
  391.6 8.8 %cholesky.17 = f32[96,96]{1,0:T(8,128)S(1)} custom-call(f32[96,96]{1,0:T(8,128)S(1)} %fusion.82), custom_call_target="Cholesky" | custom-call | tf_op jit(solution)/shard_map/jit(cholesky)/cholesky | solution.py:69
  401.7 7.4 %custom-call.7 = f32[1,96,96]{1,2,0:T(8,128)S(1)} custom-call(f32[1,96,96]{2,1,0:T(8,128)S(1)} %fusion.79), custom_call_target="InvertDiagBlocksLowerTriangular" | custom-call | tf_op jit(solution)/shard_map/jit(_solve_triangular)/triangular_solve | solution.py:70
  409.9 6.9 %all-to-all-start = ((f32[8,96,12]{1,2,0:T(8,128)}), f32[8,96,12]{1,2,0:T(8,128)S(1)}, u32[]{:S(2)}, u32[]{:S(2)}) async-start(f32[8,96,12]{1,2,0:T(8,128)} %stack.2), calls=%async_computation | async-start | bytes 131072 | tf_op jit(solution)/shard_map/all_to_all | solution.py:109
  418.5 4.7 %all-to-all-done = f32[8,96,12]{1,2,0:T(8,128)S(1)} async-done(((f32[8,96,12]{1,2,0:T(8,128)}), f32[8,96,12]{1,2,0:T(8,128)S(1)}, u32[]{:S(2)}, u32[]{:S(2)}) %all-to-all-start) | async-done | bytes 36896 | tf_op jit(solution)/shard_map/all_to_all | solution.py:109
  (46 shorter events, 18.2 us)
Async XLA Ops:
  7.2 136.6 %all-gather.3.cloned.1.call-start = ((), (), s32[]{:S(2)}) async-start(), calls=%async_computation.1 | async-start | bytes 1769472 | tf_op jit(solution)/shard_map/all_gather | solution.py:99
  8.0 15.3 %copy-start = (bf16[12,1,64,128]{3,2,1,0:T(8,128)(2,1)S(1)}, bf16[12,1,64,128]{3,2,1,0:T(8,128)(2,1)}, u32[]{:S(2)}) copy-start(bf16[12,1,64,128]{3,2,1,0:T(8,128)(2,1)} %param.4) | copy-start | bytes 589828
  9.0 13.5 %collective-permute-start.1 = (f32[12,1,64,128]{3,2,1,0:T(8,128)S(1)}, f32[12,1,64,128]{3,2,1,0:T(8,128)S(1)}, u32[]{:S(2)}, u32[]{:S(2)}) collective-permute-start(f32[12,1,64,128]{3,2,1,0:T(8,128)S(1)} %convert_multiply_fusion), channel_id=1, source_target_pairs={{0,8},{8,16},{16,24},{24,32},{32,40},{40,48},{48,56},{56,64},{64,7... | collective-permute-start | bytes 1179656 | tf_op jit(solution)/shard_map/ppermute | solution.py:18
  10.8 11.7 %collective-permute-start.3 = (f32[12,1,64,128]{3,2,1,0:T(8,128)S(1)}, f32[12,1,64,128]{3,2,1,0:T(8,128)S(1)}, u32[]{:S(2)}, u32[]{:S(2)}) collective-permute-start(f32[12,1,64,128]{3,2,1,0:T(8,128)S(1)} %convert_multiply_fusion), channel_id=1, source_target_pairs={{8,0},{16,8},{24,16},{32,24},{40,32},{48,40},{56,48},{64,56},{72,6... | collective-permute-start | bytes 1179656 | tf_op jit(solution)/shard_map/ppermute | solution.py:19
  12.9 6.9 %collective-permute-start = (f32[1,64,128]{2,1,0:T(8,128)S(1)}, f32[1,64,128]{2,1,0:T(8,128)S(1)}, u32[]{:S(2)}, u32[]{:S(2)}) collective-permute-start(f32[1,64,128]{2,1,0:T(8,128)S(1)} %select_add_fusion), channel_id=1, source_target_pairs={{0,8},{8,16},{16,24},{24,32},{32,40},{40,48},{48,56},{56,64},{64,7... | collective-permute-start | bytes 98312 | tf_op jit(solution)/shard_map/ppermute | solution.py:18
  17.1 4.3 %collective-permute-start.2 = (f32[1,64,128]{2,1,0:T(8,128)S(1)}, f32[1,64,128]{2,1,0:T(8,128)S(1)}, u32[]{:S(2)}, u32[]{:S(2)}) collective-permute-start(f32[1,64,128]{2,1,0:T(8,128)S(1)} %select_add_fusion), channel_id=1, source_target_pairs={{8,0},{16,8},{24,16},{32,24},{40,32},{48,40},{56,48},{64,56},{72,6... | collective-permute-start | bytes 98312 | tf_op jit(solution)/shard_map/ppermute | solution.py:19
  23.8 5.9 %collective-permute-start.4 = (f32[12,1,64,128]{3,2,1,0:T(8,128)S(1)}, f32[12,1,64,128]{3,2,1,0:T(8,128)S(1)}, u32[]{:S(2)}, u32[]{:S(2)}) collective-permute-start(f32[12,1,64,128]{3,2,1,0:T(8,128)S(1)} %fusion.66), channel_id=1, source_target_pairs={{0,8},{8,16},{16,24},{24,32},{32,40},{40,48},{48,56},{56,64},{64,7... | collective-permute-start | bytes 1179656 | tf_op jit(solution)/shard_map/ppermute | solution.py:18
  28.3 4.0 collective-permute-start.5
  33.7 10.3 %collective-permute-start.6 = (f32[12,1,64,128]{3,2,1,0:T(8,128)S(1)}, f32[12,1,64,128]{3,2,1,0:T(8,128)S(1)}, u32[]{:S(2)}, u32[]{:S(2)}) collective-permute-start(f32[12,1,64,128]{3,2,1,0:T(8,128)S(1)} %fusion.56), channel_id=1, source_target_pairs={{0,8},{8,16},{16,24},{24,32},{32,40},{40,48},{48,56},{56,64},{64,7... | collective-permute-start | bytes 1179656 | tf_op jit(solution)/shard_map/ppermute | solution.py:18
  42.7 3.6 collective-permute-start.7
  47.6 9.6 %collective-permute-start.8 = (f32[12,1,64,128]{3,2,1,0:T(8,128)S(1)}, f32[12,1,64,128]{3,2,1,0:T(8,128)S(1)}, u32[]{:S(2)}, u32[]{:S(2)}) collective-permute-start(f32[12,1,64,128]{3,2,1,0:T(8,128)S(1)} %fusion.44), channel_id=1, source_target_pairs={{0,8},{8,16},{16,24},{24,32},{32,40},{40,48},{48,56},{56,64},{64,7... | collective-permute-start | bytes 1179656 | tf_op jit(solution)/shard_map/ppermute | solution.py:18
  55.9 3.6 collective-permute-start.9
  61.5 9.6 %collective-permute-start.10 = (f32[12,1,64,128]{3,2,1,0:T(8,128)S(1)}, f32[12,1,64,128]{3,2,1,0:T(8,128)S(1)}, u32[]{:S(2)}, u32[]{:S(2)}) collective-permute-start(f32[12,1,64,128]{3,2,1,0:T(8,128)S(1)} %get-tuple-element.11), channel_id=1, source_target_pairs={{0,8},{8,16},{16,24},{24,32},{32,40},{40,48},{48,56},{56,64},{64,7... | collective-permute-start | bytes 1179656 | tf_op jit(solution)/shard_map/ppermute | solution.py:18
  69.8 3.6 collective-permute-start.11
  74.2 72.2 %copy-start.2 = (bf16[12,1,64,128]{3,2,1,0:T(8,128)(2,1)S(1)}, bf16[12,1,64,128]{3,2,1,0:T(8,128)(2,1)}, u32[]{:S(2)}) copy-start(bf16[12,1,64,128]{3,2,1,0:T(8,128)(2,1)} %get-tuple-element.10) | copy-start | bytes 589828
  143.8 273.1 %copy-start.1 = (bf16[96,1,64,128]{3,2,1,0:T(8,128)(2,1)S(1)}, bf16[96,1,64,128]{3,2,1,0:T(8,128)(2,1)}, u32[]{:S(2)}) copy-start(bf16[96,1,64,128]{3,2,1,0:T(8,128)(2,1)} %all-gather.3.cloned.1.call-done) | copy-start | bytes 4718596
  409.9 13.3 %all-to-all-start = ((f32[8,96,12]{1,2,0:T(8,128)}), f32[8,96,12]{1,2,0:T(8,128)S(1)}, u32[]{:S(2)}, u32[]{:S(2)}) async-start(f32[8,96,12]{1,2,0:T(8,128)} %stack.2), calls=%async_computation | async-start | bytes 131072 | tf_op jit(solution)/shard_map/all_to_all | solution.py:109
Sparse Core Ops, SparseCore 0:
  61.6 82.1 all-gather.2
